TPU v7x, 32 devices: a whole 2x2x4 slice. The times are simulated.
32 devices in a mesh: row: 4 (over z), col: 8 (over y, x, core).
Axes of the slice: x: 2, y: 2, z: 4, core: 2. Of those that a mesh axis runs over, the one named last changes fastest.
Arguments:
- tile_values: float32 [512, 512, 512], P(('row', 'col')), may hold values from -6 to 6
- tile_coords: int32 [512, 2], P(('row', 'col')), may hold values from 0 to 3, as said below
- tile_counts: int32 [32], P(('row', 'col')), may hold values from 4 to 16, as said below
- restrict_basis: float32 [8192, 256], P(('row', 'col')), may hold values from -0.25 to 0.25
- prolong_basis: float32 [16384, 256], P(('col', 'row')), may hold values from -0.25 to 0.25
- row_partner: int32 [8, 4], replicated, may hold values from 0 to 3, as said below
- col_partner: int32 [4, 8], replicated, may hold values from 0 to 7, as said below
Outputs:
- coarse: float32 [2048, 4096], P('row', 'col')
Inputs may be any that keep to these rules, and one draw needn't show every extreme that they name: `tile_coords`: within one device's 16 slots no two name the same (block row, block column); first entry below 4, second below 4; dead slots also hold such positions. `tile_counts`: number of leading slots of each device that are live; some device has all 16 live. `row_partner`: each row is a pairing: the partner of a part's partner is the part itself, never the part. `col_partner`: each row is a pairing: the partner of a part's partner is the part itself, never the part.
All inputs are finite; a program needn't handle non-finite values.
Results may differ from a plain program's by a relative error of at most 0.0003.
Values sent between devices are 32-bit elements; how exact they have to be, the bound alone decides.
No kernel may reach another device: no remote copies, remote signals or barrier semaphores. Data moves between devices by JAX's collectives and lax.ppermute only.
A program may use at most 128 MiB of HBM per device.

v0:
```python
import functools

import jax
import jax.numpy as jnp
from jax import lax
from jax.experimental import pallas as pl
from jax.experimental.pallas import tpu as pltpu
from jax.sharding import PartitionSpec as P

F32 = jnp.float32
BF16 = jnp.bfloat16
VMEM_BYTES = 48 * 1024 * 1024
PARAMS = pltpu.CompilerParams(vmem_limit_bytes=VMEM_BYTES)


def split(value):
    high = value.astype(BF16)
    low = (value - high.astype(F32)).astype(BF16)
    return high, low


def dot(left, right):
    return jnp.dot(left, right, preferred_element_type=F32)


def product(left_both, right_high, right_low):
    half = left_both.shape[0] // 2
    total = dot(left_both[half:], right_high)
    total = total + dot(left_both[:half], right_low)
    return total + dot(left_both[:half], right_high)


def div(value, by):
    return lax.div(value, jnp.int32(by))


def rem(value, by):
    return lax.rem(value, jnp.int32(by))


def half_of(given, me, row_partner):
    mate = row_partner[me[1], me[0]]
    return ((mate > me[0]) if given else (me[0] > mate)).astype(jnp.int32)


def left_kernel(given, half_rows, block_cols, per_step, *refs):
    me, slots, row_partner, q_ref = refs[:4]
    tile_refs = refs[4 : 4 + per_step]
    out, q_both = refs[4 + per_step :]
    group, step = pl.program_id(0), pl.program_id(1)
    width = q_both.shape[0] // 2

    @pl.when(step == 0)
    def _():
        high, low = split(q_ref[...].T)
        q_both[:width] = high
        q_both[width:] = low

    block_row = half_of(given, me, row_partner) * half_rows + group
    for index, tile_ref in enumerate(tile_refs):
        live = slots[block_row * block_cols + step * per_step + index] >= 0
        high, low = split(tile_ref[0])
        total = jnp.where(live, product(q_both[...], high, low), 0.0)
        out[index, 0], out[index, 1] = split(total)


def left_products(given, me, slots, row_partner, tiles, q_rows, half_rows, block_cols):
    _, tile_order, _ = tiles.shape
    width = q_rows.shape[1]
    per_step = 2 if block_cols % 2 == 0 else 1

    def row_of(g, me, row_partner):
        return half_of(given, me, row_partner) * half_rows + g

    def tile_spec(index):
        def tile_at(g, b, me, slots, row_partner):
            place = row_of(g, me, row_partner) * block_cols + b * per_step + index
            return jnp.maximum(slots[place], 0), 0, 0

        return pl.BlockSpec((1, tile_order, tile_order), tile_at)

    return pl.pallas_call(
        functools.partial(left_kernel, given, half_rows, block_cols, per_step),
        grid_spec=pltpu.PrefetchScalarGridSpec(
            num_scalar_prefetch=3,
            grid=(half_rows, block_cols // per_step),
            in_specs=[
                pl.BlockSpec(
                    (tile_order, width),
                    lambda g, b, me, slots, row_partner: (row_of(g, me, row_partner), 0),
                )
            ]
            + [tile_spec(index) for index in range(per_step)],
            out_specs=pl.BlockSpec(
                (per_step, 2, width, tile_order), lambda g, b, *_: (b, 0, g, 0)
            ),
            scratch_shapes=[pltpu.VMEM((2 * width, tile_order), BF16)],
        ),
        out_shape=jax.ShapeDtypeStruct((block_cols, 2, half_rows * width, tile_order), BF16),
        compiler_params=PARAMS,
        cost_estimate=pl.CostEstimate(
            flops=12 * half_rows * block_cols * width * tile_order * tile_order,
            bytes_accessed=4 * half_rows * block_cols * tile_order * (tile_order + width),
            transcendentals=0,
        ),
        name="left_products",
    )(me, slots, row_partner, q_rows, *[tiles] * per_step)


def column_of(given, block_cols, step, me, row_partner, col_partner):
    row, col = me[0], me[1]
    holder = row_partner[col, row] if given else row
    keeps = col > col_partner[holder, col]
    half_cols = block_cols // 2
    later = div(step, half_cols)
    return jnp.where(keeps, later, 1 - later) * half_cols + rem(step, half_cols)


def live_blocks(given, half_rows, block_cols, me, table, row_partner, col_partner):
    first = half_of(given, me, row_partner) * half_rows
    flags = []
    for step in range(block_cols):
        column = column_of(given, block_cols, jnp.int32(step), me, row_partner, col_partner)
        for block_row in range(half_rows):
            slot = table((first + block_row) * block_cols + column)
            flags.append((slot >= 0).astype(jnp.int32))
    return flags


def packed_place(flags, block):
    before = here = jnp.int32(0)
    for index, flag in enumerate(flags):
        before = before + jnp.where(index < block, flag, 0)
        here = here + jnp.where(index == block, flag, 0)
    return jnp.where(here == 1, before, sum(flags) + block - before), here


def right_kernel(given, block_cols, half_rows, shard_places, groups, *refs):
    me, slots, row_partner, col_partner, w_ref = refs[:5]
    pieces = refs[5 : 5 + sum(groups)]
    p_high, p_low = refs[-2:]
    step = pl.program_id(0)
    tile_order = w_ref.shape[3]
    depth, width = pieces[0].shape

    @pl.when(step == 0)
    def _():
        at = 0
        for place, count in zip(shard_places(me), groups):
            value = pieces[at][...]
            for other in range(1, count):
                value = value + pieces[at + other][...]
            at += count
            rows = pl.ds(pl.multiple_of(place * depth, depth), depth)
            p_high[rows, :], p_low[rows, :] = split(value)

    column = column_of(given, block_cols, step, me, row_partner, col_partner)
    rows = pl.ds(pl.multiple_of(column * tile_order, tile_order), tile_order)
    both = w_ref[0].reshape(2 * w_ref.shape[2], tile_order)
    block = product(both, p_high[rows, :], p_low[rows, :])
    if not given:
        first, second = refs[5 + sum(groups) : -2]
        half_cols = block_cols // 2

        @pl.when(step < half_cols)
        def _():
            first[...] = block

        @pl.when(step >= half_cols)
        def _():
            second[...] = block

        return
    outs = refs[5 + sum(groups) : -3]
    packed = refs[-3]
    flags = live_blocks(
        given, half_rows, block_cols, me, lambda place: slots[place], row_partner, col_partner
    )
    for block_row in range(half_rows):
        place, _ = packed_place(flags, step * half_rows + block_row)
        packed[place] = block[block_row * width : (block_row + 1) * width]

    @pl.when(step == block_cols - 1)
    def _():
        count = outs[0].shape[0]
        outs[0][...] = packed[:count]
        for index, out in enumerate(outs[1:]):
            out[...] = packed[count + index]


def right_products(given, me, slots, row_partner, col_partner, w, shards, shard_places, half_rows):
    block_cols, _, height, tile_order = w.shape
    half_cols = block_cols // 2
    depth, width = shards[0][0].shape
    groups = [len(shard) for shard in shards]
    blocks = half_rows * block_cols

    def w_at(i, me, slots, row_partner, col_partner):
        return column_of(given, block_cols, i, me, row_partner, col_partner), 0, 0, 0

    def out_spec(first):
        return pl.BlockSpec(
            (height, width), lambda i, *_: (0, jnp.clip(i - first, 0, half_cols - 1))
        )

    scratch = [pltpu.VMEM((len(shards) * depth, width), BF16)] * 2
    if given:
        shapes = [(blocks // 2, width, width)] + [(width, width)] * (blocks - blocks // 2)
        out_specs = [pl.BlockSpec(shape, lambda i, *_, n=len(shape): (0,) * n) for shape in shapes]
        scratch = [pltpu.VMEM((blocks, width, width), F32)] + scratch
    else:
        shapes = [(height, half_cols * width)] * 2
        out_specs = [out_spec(0), out_spec(half_cols)]
    whole = pl.BlockSpec(memory_space=pltpu.VMEM)
    return pl.pallas_call(
        functools.partial(right_kernel, given, block_cols, half_rows, shard_places, groups),
        grid_spec=pltpu.PrefetchScalarGridSpec(
            num_scalar_prefetch=4,
            grid=(block_cols,),
            in_specs=[pl.BlockSpec((1, 2, height, tile_order), w_at)] + [whole] * sum(groups),
            out_specs=out_specs,
            scratch_shapes=scratch,
        ),
        out_shape=[jax.ShapeDtypeStruct(shape, F32) for shape in shapes],
        compiler_params=PARAMS,
        cost_estimate=pl.CostEstimate(
            flops=6 * block_cols * height * width * tile_order,
            bytes_accessed=4 * block_cols * height * (tile_order + width),
            transcendentals=0,
        ),
        name="right_products",
    )(me, slots, row_partner, col_partner, w, *[piece for shard in shards for piece in shard])


def sum_kernel(source, first, *refs):
    tables, kept_ref, packed_ref = refs[:4], refs[4], refs[5]
    singles, out = refs[6 : 6 + source.singles], refs[-1]
    place, live = source.place(first + pl.program_id(0), *tables)
    total = kept_ref[...]
    if len(refs) > 7 + source.singles:
        total = total + refs[-2][...]
    out[...] = total + jnp.where((live == 1) & (place < source.packed), packed_ref[0], 0.0)
    for index, single in enumerate(singles):

        @pl.when((live == 1) & (place == source.packed + index))
        def _():
            out[...] = total + single[...]


class PackedSource:
    def __init__(self, half_rows, block_cols):
        self.half_rows = half_rows
        self.block_cols = block_cols
        blocks = half_rows * block_cols
        self.packed = blocks // 2
        self.singles = blocks - self.packed

    def place(self, block, me, mate_slots, row_partner, col_partner):
        flags = live_blocks(
            False,
            self.half_rows,
            self.block_cols,
            me,
            lambda place: mate_slots[place],
            row_partner,
            col_partner,
        )
        return packed_place(flags, block)


def sum_blocks(second, tables, source, kept, packed, singles, section=None):
    height, both = kept.shape
    width = packed.shape[1]
    half_rows, half_cols = source.half_rows, source.block_cols // 2
    first = half_rows * half_cols if second else 0

    def packed_at(i, *tables):
        place, _ = source.place(first + i, *tables)
        return jnp.minimum(place, source.packed - 1), 0, 0

    block = pl.BlockSpec(
        (width, width), lambda i, *_: (rem(i, half_rows), div(i, half_rows))
    )
    sections = [] if section is None else [section]
    return pl.pallas_call(
        functools.partial(sum_kernel, source, first),
        grid_spec=pltpu.PrefetchScalarGridSpec(
            num_scalar_prefetch=4,
            grid=(half_rows * half_cols,),
            in_specs=[block, pl.BlockSpec((1, width, width), packed_at)]
            + [pl.BlockSpec(memory_space=pltpu.VMEM)] * len(singles)
            + [block] * len(sections),
            out_specs=block,
        ),
        out_shape=jax.ShapeDtypeStruct((height, both), F32),
        compiler_params=PARAMS,
        name="sum_blocks",
    )(*tables, kept, packed, *singles, *sections)


def flip(value, axis, size, mask):
    return lax.ppermute(value, axis, [(i, i ^ mask) for i in range(size)])


def gather_prolong(shard, axis, size):
    if size != 4:
        gathered = lax.all_gather(shard, axis)
        return [[gathered[i]] for i in range(size)], lambda me: list(range(size))
    by_two = flip(shard, axis, size, 2)
    by_one = flip(shard, axis, size, 1)
    middle = lax.ppermute(shard, axis, [(1, 2), (2, 1)])
    handed = lax.ppermute(by_two, axis, [(1, 0), (2, 3)])
    return [[shard], [by_one], [by_two], [middle, handed]], lambda me: [me[0] ^ m for m in range(4)]


def pair_switch(mine, mate, size, branch, operand, sizes=(None,), choice=0):
    branches = [functools.partial(branch, mask, each) for mask in range(1, size) for each in sizes]
    if len(branches) == 1:
        return branches[0](operand)
    return lax.switch(((mine ^ mate) - 1) * len(sizes) + choice, branches, operand)


def solution(mesh):
    n_row = mesh.shape["row"]
    n_col = mesh.shape["col"]

    def body(tiles, coords, counts, restrict, prolong, row_partner, col_partner):
        tile_order = tiles.shape[1]
        block_rows = restrict.shape[0] * n_col // tile_order
        block_cols = prolong.shape[0] * n_row // tile_order
        half_rows, half_cols = block_rows // 2, block_cols // 2
        row = lax.axis_index("row").astype(jnp.int32)
        col = lax.axis_index("col").astype(jnp.int32)
        me = jnp.stack([row, col])

        q_rows = lax.all_gather(restrict, "col", axis=0, tiled=True)
        shards, shard_places = gather_prolong(prolong, "row", n_row)

        slot_ids = jnp.arange(tiles.shape[0], dtype=jnp.int32)
        place_ids = jnp.arange(block_rows * block_cols, dtype=jnp.int32)
        named = (coords[:, 0] * block_cols + coords[:, 1])[None, :] == place_ids[:, None]
        hit = named & (slot_ids < counts[0])[None, :]
        slots = jnp.max(jnp.where(hit, slot_ids[None, :], -1), axis=1)

        def half_grid(given):
            w = left_products(given, me, slots, row_partner, tiles, q_rows, half_rows, block_cols)
            return right_products(
                given, me, slots, row_partner, col_partner, w, shards, shard_places, half_rows
            )

        def swap(mask, _, chunk):
            return flip(chunk, "row", n_row, mask)

        def swap_first(mask, _, chunk):
            return flip(chunk, "row", n_row, mask), half_grid(False)

        def swap_some(mask, count, singles):
            return [
                flip(single, "row", n_row, mask) if index < count else single
                for index, single in enumerate(singles)
            ]

        def swap_section(mask, _, section):
            return flip(section, "col", n_col, mask)

        row_mate = row_partner[col, row]
        col_mate = col_partner[row, col]

        mate_slots = pair_switch(row, row_mate, n_row, swap, slots)
        upper = place_ids >= half_rows * block_cols
        mine = (slots >= 0) & (upper == (row < row_mate))
        mates = (mate_slots >= 0) & (upper == (row > row_mate))
        most = jnp.maximum(mine.astype(jnp.int32).sum(), mates.astype(jnp.int32).sum())
        extra = jnp.maximum(most - (half_rows * block_cols) // 2, 0)

        packed, *singles = half_grid(True)

        packed, extra = lax.optimization_barrier((packed, extra))
        packed, kept = pair_switch(row, row_mate, n_row, swap_first, packed)
        counts = tuple(range(len(singles) + 1))
        singles, packed = lax.optimization_barrier((singles, packed))
        singles = pair_switch(row, row_mate, n_row, swap_some, singles, counts, extra)
        tables = (me, mate_slots, row_partner, col_partner)
        source = PackedSource(half_rows, block_cols)
        section = sum_blocks(False, tables, source, kept[0], packed, singles)
        section = pair_switch(col, col_mate, n_col, swap_section, section)
        return sum_blocks(True, tables, source, kept[1], packed, singles, section)

    in_specs = (
        P(("row", "col"), None, None),
        P(("row", "col"), None),
        P(("row", "col")),
        P(("row", "col"), None),
        P(("col", "row"), None),
        P(),
        P(),
    )
    return jax.shard_map(
        body, mesh=mesh, in_specs=in_specs, out_specs=P("row", "col"), check_vma=False
    )
```

profile of v0, /device:TPU:11, one launch (start us, length us, event | category | flops | bytes accessed | tf_op | source)
XLA Modules:
  0.0 195.7 jit_solution(1870596405740009371)
XLA Ops:
  6.5 0.7 all-gather.2.cloned.1.call-update
  7.3 2.4 %collective-permute-start.44 = (f32[512,256]{1,0:T(8,128)}, f32[512,256]{1,0:T(8,128)S(1)}, u32[]{:S(2)}, u32[]{:S(2)}) collective-permute-start(f32[512,256]{1,0:T(8,128)} %refs_5_.3), channel_id=1, source_target_pairs={{0,16},{8,24},{16,0},{24,8},{1,17},{9,25},{17,1},{25,9},{2,18},{10... | collective-permute-start | bytes 1572872 | tf_op jit(solution)/shard_map/ppermute | solution.py:302
  9.8 2.1 %collective-permute-start.45 = (f32[512,256]{1,0:T(8,128)}, f32[512,256]{1,0:T(8,128)}, u32[]{:S(2)}, u32[]{:S(2)}) collective-permute-start(f32[512,256]{1,0:T(8,128)} %refs_5_.3), channel_id=1, source_target_pairs={{8,16},{16,8},{9,17},{17,9},{10,18},{18,10},{11,19},{19,11},{12,20... | collective-permute-start | bytes 1572872 | tf_op jit(solution)/shard_map/ppermute | solution.py:311
  11.9 1.3 dynamic_slice.6
  14.9 0.8 copy.21.refs_2_
  16.3 0.8 add_bitcast_fusion
  17.2 26.8 %conditional.4 = (s32[16]{0:T(128)}) conditional(s32[]{:T(128)} %clamp.10, s32[16]{0:T(128)S(1)} %select_reduce_fusion.refs_1_, s32[16]{0:T(128)S(1)} %select_reduce_fusion.refs_1_, s32[16]{0:T(128)S(1)} %select_reduce_fusion.refs_1_), branch_computations={%region_1.2_spmd, %region_2.3_spmd, %region_3.4_spmd} | conditional | bytes 304 | solution.py:320
  17.2 1.3 collective-permute-start.2
  18.5 25.4 %collective-permute-done.2 = s32[16]{0:T(128)} collective-permute-done((s32[16]{0:T(128)S(1)}, s32[16]{0:T(128)}, u32[]{:S(2)}, u32[]{:S(2)}) %collective-permute-start.2) | collective-permute-done | bytes 96 | tf_op jit(solution)/shard_map/cond/branch_2_fun/ppermute | solution.py:302
  44.0 1.2 fusion.1
  46.4 1.3 dynamic_slice.7
  48.3 2.2 %collective-permute-start.46 = (f32[512,256]{1,0:T(8,128)S(1)}, f32[512,256]{1,0:T(8,128)}, u32[]{:S(2)}, u32[]{:S(2)}) collective-permute-start(f32[512,256]{1,0:T(8,128)S(1)} %collective-permute-done.44.refs_7_), channel_id=1, source_target_pairs={{8,0},{16,24},{9,1},{17,25},{10,2},{18,26},{11,3},{19,27},{12,4},{... | collective-permute-start | bytes 1572872 | tf_op jit(solution)/shard_map/ppermute | solution.py:312
  50.5 7.9 %left_products.7.refs_4_ = bf16[4,2,512,512]{3,2,1,0:T(8,128)(2,1)S(1)} custom-call(s32[2]{0:T(128)S(1)} %pad_add_fusion.refs_0_, s32[16]{0:T(128)S(1)} %select_reduce_fusion.refs_1_, s32[8,4]{1,0:T(8,128)S(1)} %copy.21.refs_2_, f32[2048,256]{1,0:T(8,128)} %all-gather.2.cloned.1.call-done.refs_3_, f32[16,512,512]{2,1,0:T(8,128)} %refs_5_.2, ...), custom_call_target="tpu_custom_call" | custom-call | flops 6442450944 | bytes 12582912 | tf_op jit(solution)/shard_map/left_products/pallas_call | solution.py:82
  58.5 2.3 %collective-permute-done.46.refs_9_ = f32[512,256]{1,0:T(8,128)} collective-permute-done((f32[512,256]{1,0:T(8,128)S(1)}, f32[512,256]{1,0:T(8,128)}, u32[]{:S(2)}, u32[]{:S(2)}) %collective-permute-start.46) | collective-permute-done | bytes 524320 | tf_op jit(solution)/shard_map/ppermute | solution.py:312
  60.8 6.3 %right_products.7 = (f32[4,256,256]{2,1,0:T(8,128)}, f32[256,256]{1,0:T(8,128)}, f32[256,256]{1,0:T(8,128)}, f32[256,256]{1,0:T(8,128)}, f32[256,256]{1,0:T(8,128)S(1)}) custom-call(s32[2]{0:T(128)S(1)} %pad_add_fusion.refs_0_, s32[16]{0:T(128)S(1)} %select_reduce_fusion.refs_1_, s32[8,4]{1,0:T(8,128)S(1)} %copy.21.refs_2_, s32[4,8]{1,0:T(4,128)S(1)} %copy-done.5, ...), custom_call_target="tpu_custom_call" | custom-call | flops 1610612736 | bytes 6291456 | tf_op jit(solution)/shard_map/right_products/pallas_call | solution.py:215
  67.1 67.1 %conditional.5 = (f32[4,256,256]{2,1,0:T(8,128)}, f32[512,512]{1,0:T(8,128)S(1)}, f32[512,512]{1,0:T(8,128)S(1)}) conditional(s32[]{:T(128)} %clamp.10, (f32[4,256,256]{2,1,0:T(8,128)}, s32[2]{0:T(128)S(1)}, s32[16]{0:T(128)S(1)}, s32[8,4]{0,1:T(4,128)S(1)}, f32[2048,256]{1,0:T(8,128)S(1)}, /*index=5*/f32[16,512,512]{2,1,0:T(8,128)}, ...), branch_computations={%region_6.7_spmd, %region_7.8_spmd, %region_8.9_spmd} | conditional | flops 8053063680 | bytes 23068992 | solution.py:320
  67.1 2.2 %collective-permute-start.5 = (f32[4,256,256]{2,1,0:T(8,128)}, f32[4,256,256]{2,1,0:T(8,128)}, u32[]{:S(2)}, u32[]{:S(2)}) collective-permute-start(f32[4,256,256]{2,1,0:T(8,128)} %get-tuple-element.247), channel_id=1, source_target_pairs={{0,24},{8,16},{16,8},{24,0},{1,25},{9,17},{17,9},{25,1},{2,26},{10... | collective-permute-start | bytes 3145736 | tf_op jit(solution)/shard_map/cond/branch_2_fun/ppermute | solution.py:302
  69.4 7.6 %left_products.6.refs_4_ = bf16[4,2,512,512]{3,2,1,0:T(8,128)(2,1)S(1)} custom-call(s32[2]{0:T(128)S(1)} %get-tuple-element.248.refs_0_, s32[16]{0:T(128)S(1)} %get-tuple-element.249.refs_1_, s32[8,4]{1,0:T(8,128)S(1)} %copy.19.refs_2_, f32[2048,256]{1,0:T(8,128)S(1)} %get-tuple-element.252.refs_3_, f32[16,512,512]{2,1,0:T(8,128)} %get-tuple-element.253.refs_4_.refs_5_, ...), custom_call_target="tpu_custom_call" | custom-call | flops 6442450944 | bytes 12582912 | tf_op jit(solution)/shard_map/cond/branch_2_fun/left_products/pallas_call | solution.py:82
  76.9 5.2 %right_products.6 = (f32[512,512]{1,0:T(8,128)S(1)}, f32[512,512]{1,0:T(8,128)S(1)}) custom-call(s32[2]{0:T(128)S(1)} %get-tuple-element.248.refs_0_, s32[16]{0:T(128)S(1)} %get-tuple-element.249.refs_1_, s32[8,4]{1,0:T(8,128)S(1)} %copy.19.refs_2_, s32[4,8]{1,0:T(4,128)S(1)} %get-tuple-element.251.refs_3_, ...), custom_call_target="tpu_custom_call" | custom-call | flops 1610612736 | bytes 6291456 | tf_op jit(solution)/shard_map/cond/branch_2_fun/right_products/pallas_call | solution.py:215
  82.1 52.0 %collective-permute-done.5 = f32[4,256,256]{2,1,0:T(8,128)} collective-permute-done((f32[4,256,256]{2,1,0:T(8,128)}, f32[4,256,256]{2,1,0:T(8,128)}, u32[]{:S(2)}, u32[]{:S(2)}) %collective-permute-start.5) | collective-permute-done | bytes 1048608 | tf_op jit(solution)/shard_map/cond/branch_2_fun/ppermute | solution.py:302
  134.1 23.2 %conditional.6 = ((f32[256,256]{1,0:T(8,128)}, f32[256,256]{1,0:T(8,128)}, f32[256,256]{1,0:T(8,128)}, f32[256,256]{1,0:T(8,128)S(1)})) conditional(s32[]{:T(128)} %clamp.11, (f32[256,256]{1,0:T(8,128)}, f32[256,256]{1,0:T(8,128)}, f32[256,256]{1,0:T(8,128)}, f32[256,256]{1,0:T(8,128)S(1)}) %tuple.109, ...), branch_computations={%region_9.10_spmd, %region_10.11_spmd, %region_11.12_spmd, %region... | conditional | bytes 6291656 | solution.py:320
  134.1 1.2 collective-permute-start.32
  135.6 1.2 collective-permute-start.34
  137.1 3.4 %collective-permute-done.32 = f32[256,256]{1,0:T(8,128)S(1)} collective-permute-done((f32[256,256]{1,0:T(8,128)}, f32[256,256]{1,0:T(8,128)S(1)}, u32[]{:S(2)}, u32[]{:S(2)}) %collective-permute-start.32) | collective-permute-done | bytes 262176 | tf_op jit(solution)/shard_map/cond/branch_14_fun/ppermute | solution.py:302
  141.1 4.9 %collective-permute-done.33 = f32[256,256]{1,0:T(8,128)S(1)} collective-permute-done((f32[256,256]{1,0:T(8,128)}, f32[256,256]{1,0:T(8,128)S(1)}, u32[]{:S(2)}, u32[]{:S(2)}) %collective-permute-start.33) | collective-permute-done | bytes 262176 | tf_op jit(solution)/shard_map/cond/branch_14_fun/ppermute | solution.py:302
  146.0 0.7 copy.91
  146.8 4.9 %collective-permute-done.34 = f32[256,256]{1,0:T(8,128)S(1)} collective-permute-done((f32[256,256]{1,0:T(8,128)}, f32[256,256]{1,0:T(8,128)S(1)}, u32[]{:S(2)}, u32[]{:S(2)}) %collective-permute-start.34) | collective-permute-done | bytes 262176 | tf_op jit(solution)/shard_map/cond/branch_14_fun/ppermute | solution.py:302
  152.4 4.9 %collective-permute-done.35 = f32[256,256]{1,0:T(8,128)S(1)} collective-permute-done((f32[256,256]{1,0:T(8,128)S(1)}, f32[256,256]{1,0:T(8,128)S(1)}, u32[]{:S(2)}, u32[]{:S(2)}) %collective-permute-start.35) | collective-permute-done | bytes 262176 | tf_op jit(solution)/shard_map/cond/branch_14_fun/ppermute | solution.py:302
  157.3 3.8 %sum_blocks.2 = f32[512,512]{1,0:T(8,128)S(1)} custom-call(s32[2]{0:T(128)S(1)} %pad_add_fusion.refs_0_, s32[16]{0:T(128)} %get-tuple-element.490.refs_1_, s32[8,4]{1,0:T(8,128)S(1)} %copy.21.refs_2_, s32[4,8]{1,0:T(4,128)S(1)} %copy-done.5, f32[512,512]{1,0:T(8,128)S(1)} %get-tuple-element.346.refs_4_, f32[4,256,256]{2,1,0:T(8,128)} %get-tuple-element.336.refs_5_, ...), custom_call_target="tpu_custom_call" | custom-call | tf_op jit(solution)/shard_map/sum_blocks/pallas_call | solution.py:285
  161.2 23.1 %conditional.7 = (f32[512,512]{1,0:T(8,128)}) conditional(s32[]{:T(128)} %clamp.12, f32[512,512]{1,0:T(8,128)S(1)} %sum_blocks.2, f32[512,512]{1,0:T(8,128)S(1)} %sum_blocks.2, f32[512,512]{1,0:T(8,128)S(1)} %sum_blocks.2, f32[512,512]{1,0:T(8,128)S(1)} %sum_blocks.2, f32[512,512]{1,0:T(8,128)S(1)} %sum_blocks.2, ...), branch_computations={%region_24.25_spmd, %region_25.26_spmd, %region_26.27_spmd, %regio... | conditional | bytes 4194352 | solution.py:320
  161.3 23.0 %collective-permute-done.41 = f32[512,512]{1,0:T(8,128)} collective-permute-done((f32[512,512]{1,0:T(8,128)S(1)}, f32[512,512]{1,0:T(8,128)}, u32[]{:S(2)}, u32[]{:S(2)}) %collective-permute-start.41) | collective-permute-done | bytes 1048608 | tf_op jit(solution)/shard_map/cond/branch_5_fun/ppermute | solution.py:302
  184.3 4.6 %sum_blocks.3 = f32[512,512]{1,0:T(8,128)} custom-call(s32[2]{0:T(128)S(1)} %pad_add_fusion.refs_0_, s32[16]{0:T(128)} %get-tuple-element.490.refs_1_, s32[8,4]{1,0:T(8,128)S(1)} %copy.21.refs_2_, s32[4,8]{1,0:T(4,128)S(1)} %copy-done.5, f32[512,512]{1,0:T(8,128)S(1)} %get-tuple-element.330.refs_4_, f32[4,256,256]{2,1,0:T(8,128)} %get-tuple-element.336.refs_5_, ...), custom_call_target="tpu_custom_call" | custom-call | tf_op jit(solution)/shard_map/sum_blocks/pallas_call | solution.py:285
  (30 shorter events, 2.6 us)
Async XLA Ops:
  6.5 44.0 %all-gather.2.cloned.1.call-start = ((), (), s32[]{:S(2)}) async-start(), calls=%async_computation | async-start | bytes 2359296 | tf_op jit(solution)/shard_map/all_gather | solution.py:336
  7.3 41.0 %collective-permute-start.44 = (f32[512,256]{1,0:T(8,128)}, f32[512,256]{1,0:T(8,128)S(1)}, u32[]{:S(2)}, u32[]{:S(2)}) collective-permute-start(f32[512,256]{1,0:T(8,128)} %refs_5_.3), channel_id=1, source_target_pairs={{0,16},{8,24},{16,0},{24,8},{1,17},{9,25},{17,1},{25,9},{2,18},{10... | collective-permute-start | bytes 1572872 | tf_op jit(solution)/shard_map/ppermute | solution.py:302
  9.6 48.9 %collective-permute-start.43 = (f32[512,256]{1,0:T(8,128)}, f32[512,256]{1,0:T(8,128)}, u32[]{:S(2)}, u32[]{:S(2)}) collective-permute-start(f32[512,256]{1,0:T(8,128)} %refs_5_.3), channel_id=1, source_target_pairs={{0,8},{8,0},{16,24},{24,16},{1,9},{9,1},{17,25},{25,17},{2,10},{10... | collective-permute-start | bytes 1572872 | tf_op jit(solution)/shard_map/ppermute | solution.py:302
  9.8 48.7 %collective-permute-start.45 = (f32[512,256]{1,0:T(8,128)}, f32[512,256]{1,0:T(8,128)}, u32[]{:S(2)}, u32[]{:S(2)}) collective-permute-start(f32[512,256]{1,0:T(8,128)} %refs_5_.3), channel_id=1, source_target_pairs={{8,16},{16,8},{9,17},{17,9},{10,18},{18,10},{11,19},{19,11},{12,20... | collective-permute-start | bytes 1572872 | tf_op jit(solution)/shard_map/ppermute | solution.py:311
  17.2 26.7 %collective-permute-start.2 = (s32[16]{0:T(128)S(1)}, s32[16]{0:T(128)}, u32[]{:S(2)}, u32[]{:S(2)}) collective-permute-start(s32[16]{0:T(128)S(1)} %param.2), channel_id=1, source_target_pairs={{0,24},{8,16},{16,8},{24,0},{1,25},{9,17},{17,9},{25,1},{2,26},{10... | collective-permute-start | bytes 200 | tf_op jit(solution)/shard_map/cond/branch_2_fun/ppermute | solution.py:302
  48.3 12.5 %copy-start.1 = (f32[512,256]{1,0:T(8,128)S(1)}, f32[512,256]{1,0:T(8,128)}, u32[]{:S(2)}) copy-start(f32[512,256]{1,0:T(8,128)} %refs_5_.3) | copy-start | bytes 1572868
  48.3 12.5 %copy-start.5 = (s32[4,8]{1,0:T(4,128)S(1)}, s32[4,8]{1,0:T(4,128)}, u32[]{:S(2)}) copy-start(s32[4,8]{1,0:T(4,128)} %refs_3_.5) | copy-start | bytes 388
  48.3 12.5 %collective-permute-start.46 = (f32[512,256]{1,0:T(8,128)S(1)}, f32[512,256]{1,0:T(8,128)}, u32[]{:S(2)}, u32[]{:S(2)}) collective-permute-start(f32[512,256]{1,0:T(8,128)S(1)} %collective-permute-done.44.refs_7_), channel_id=1, source_target_pairs={{8,0},{16,24},{9,1},{17,25},{10,2},{18,26},{11,3},{19,27},{12,4},{... | collective-permute-start | bytes 1572872 | tf_op jit(solution)/shard_map/ppermute | solution.py:312
  58.5 8.6 %copy-start = (f32[2048,256]{1,0:T(8,128)S(1)}, f32[2048,256]{1,0:T(8,128)}, u32[]{:S(2)}) copy-start(f32[2048,256]{1,0:T(8,128)} %all-gather.2.cloned.1.call-done.refs_3_) | copy-start | bytes 6291460
  58.5 8.6 %copy-start.6 = (s32[8,4]{0,1:T(4,128)S(1)}, s32[8,4]{0,1:T(4,128)}, u32[]{:S(2)}) copy-start(s32[8,4]{0,1:T(4,128)} %param.40) | copy-start | bytes 388
  67.1 67.0 %collective-permute-start.5 = (f32[4,256,256]{2,1,0:T(8,128)}, f32[4,256,256]{2,1,0:T(8,128)}, u32[]{:S(2)}, u32[]{:S(2)}) collective-permute-start(f32[4,256,256]{2,1,0:T(8,128)} %get-tuple-element.247), channel_id=1, source_target_pairs={{0,24},{8,16},{16,8},{24,0},{1,25},{9,17},{17,9},{25,1},{2,26},{10... | collective-permute-start | bytes 3145736 | tf_op jit(solution)/shard_map/cond/branch_2_fun/ppermute | solution.py:302
  134.1 6.3 %collective-permute-start.32 = (f32[256,256]{1,0:T(8,128)}, f32[256,256]{1,0:T(8,128)S(1)}, u32[]{:S(2)}, u32[]{:S(2)}) collective-permute-start(f32[256,256]{1,0:T(8,128)} %get-tuple-element.305), channel_id=1, source_target_pairs={{0,24},{8,16},{16,8},{24,0},{1,25},{9,17},{17,9},{25,1},{2,26},{10... | collective-permute-start | bytes 786440 | tf_op jit(solution)/shard_map/cond/branch_14_fun/ppermute | solution.py:302
  135.3 10.8 %collective-permute-start.33 = (f32[256,256]{1,0:T(8,128)}, f32[256,256]{1,0:T(8,128)S(1)}, u32[]{:S(2)}, u32[]{:S(2)}) collective-permute-start(f32[256,256]{1,0:T(8,128)} %get-tuple-element.306), channel_id=1, source_target_pairs={{0,24},{8,16},{16,8},{24,0},{1,25},{9,17},{17,9},{25,1},{2,26},{10... | collective-permute-start | bytes 786440 | tf_op jit(solution)/shard_map/cond/branch_14_fun/ppermute | solution.py:302
  135.6 16.1 %collective-permute-start.34 = (f32[256,256]{1,0:T(8,128)}, f32[256,256]{1,0:T(8,128)S(1)}, u32[]{:S(2)}, u32[]{:S(2)}) collective-permute-start(f32[256,256]{1,0:T(8,128)} %get-tuple-element.307), channel_id=1, source_target_pairs={{0,24},{8,16},{16,8},{24,0},{1,25},{9,17},{17,9},{25,1},{2,26},{10... | collective-permute-start | bytes 786440 | tf_op jit(solution)/shard_map/cond/branch_14_fun/ppermute | solution.py:302
  136.8 20.5 %collective-permute-start.35 = (f32[256,256]{1,0:T(8,128)S(1)}, f32[256,256]{1,0:T(8,128)S(1)}, u32[]{:S(2)}, u32[]{:S(2)}) collective-permute-start(f32[256,256]{1,0:T(8,128)S(1)} %get-tuple-element.308), channel_id=1, source_target_pairs={{0,24},{8,16},{16,8},{24,0},{1,25},{9,17},{17,9},{25,1},{2,26},{10... | collective-permute-start | bytes 786440 | tf_op jit(solution)/shard_map/cond/branch_14_fun/ppermute | solution.py:302
  157.3 27.0 %copy-start.2 = (f32[256,256]{1,0:T(8,128)S(1)}, f32[256,256]{1,0:T(8,128)}, u32[]{:S(2)}) copy-start(f32[256,256]{1,0:T(8,128)} %get-tuple-element.344.refs_8_) | copy-start | bytes 786436
  157.3 27.0 %copy-start.3 = (f32[256,256]{1,0:T(8,128)S(1)}, f32[256,256]{1,0:T(8,128)}, u32[]{:S(2)}) copy-start(f32[256,256]{1,0:T(8,128)} %get-tuple-element.343.refs_7_) | copy-start | bytes 786436
  157.3 27.0 %copy-start.4 = (f32[256,256]{1,0:T(8,128)S(1)}, f32[256,256]{1,0:T(8,128)}, u32[]{:S(2)}) copy-start(f32[256,256]{1,0:T(8,128)} %get-tuple-element.342.refs_6_) | copy-start | bytes 786436
  161.2 23.1 %collective-permute-start.41 = (f32[512,512]{1,0:T(8,128)S(1)}, f32[512,512]{1,0:T(8,128)}, u32[]{:S(2)}, u32[]{:S(2)}) collective-permute-start(f32[512,512]{1,0:T(8,128)S(1)} %param.26), channel_id=1, source_target_pairs={{0,6},{1,7},{2,4},{3,5},{4,2},{5,3},{6,0},{7,1},{8,14},{9,15},{10,... | collective-permute-start | bytes 3145736 | tf_op jit(solution)/shard_map/cond/branch_5_fun/ppermute | solution.py:302
Sparse Core Ops, SparseCore 0:
  9.2 29.4 all-gather.1
where the time goes:
time: 198 us; the launch traced here: 196 us
  waiting for transfers between devices  122 us (62%)
  Pallas kernels  35.4 us (18%)
  between operations  17.6 us (9%)
  starting transfers between devices  13.4 us (7%)
  local copies, waits for them, and re-layouts  5.55 us (3%)
  other arithmetic  2.18 us (1%)
    ppermute x9, waiting for transfers between devices, flip(): return lax.ppermute(value, axis, [(i, i ^ mask) for i in range(size)])  119 us
    pallas_call x2, Pallas kernels, left_products(): pl.pallas_call(functools.partial(left_kernel, given, half_rows, block_col...  15.5 us
    pallas_call x2, Pallas kernels, right_products(): pl.pallas_call(functools.partial(right_kernel, given, block_cols, half_ro...  11.4 us
    ppermute x9, starting transfers between devices, flip(): return lax.ppermute(value, axis, [(i, i ^ mask) for i in range(size)])  9.08 us
    pallas_call x2, Pallas kernels, sum_blocks(): pl.pallas_call(functools.partial(sum_kernel, source, first), grid_spec=pl...  8.42 us
  transfers between devices with their start and end apart: 12, of which 8 were waited for; matrix products, arithmetic and copies ran while one was open for 4% of the time, Pallas kernels for 11%

commit v1 on v0

--- a/solution.py
+++ b/solution.py
@@ -232,13 +232,13 @@
     )(me, slots, row_partner, col_partner, w, *[piece for shard in shards for piece in shard])
 
 
-def sum_kernel(source, first, *refs):
+def sum_kernel(source, first, singles, *refs):
     tables, kept_ref, packed_ref = refs[:4], refs[4], refs[5]
-    singles, out = refs[6 : 6 + source.singles], refs[-1]
+    singles, sections, out = refs[6 : 6 + singles], refs[6 + singles : -1], refs[-1]
     place, live = source.place(first + pl.program_id(0), *tables)
     total = kept_ref[...]
-    if len(refs) > 7 + source.singles:
-        total = total + refs[-2][...]
+    for section in sections:
+        total = total + section[...]
     out[...] = total + jnp.where((live == 1) & (place < source.packed), packed_ref[0], 0.0)
     for index, single in enumerate(singles):
 
@@ -251,9 +251,7 @@
     def __init__(self, half_rows, block_cols):
         self.half_rows = half_rows
         self.block_cols = block_cols
-        blocks = half_rows * block_cols
-        self.packed = blocks // 2
-        self.singles = blocks - self.packed
+        self.packed = half_rows * block_cols // 2
 
     def place(self, block, me, mate_slots, row_partner, col_partner):
         flags = live_blocks(
@@ -283,7 +281,7 @@
     )
     sections = [] if section is None else [section]
     return pl.pallas_call(
-        functools.partial(sum_kernel, source, first),
+        functools.partial(sum_kernel, source, first, len(singles)),
         grid_spec=pltpu.PrefetchScalarGridSpec(
             num_scalar_prefetch=4,
             grid=(half_rows * half_cols,),
@@ -348,11 +346,15 @@
                 given, me, slots, row_partner, col_partner, w, shards, shard_places, half_rows
             )
 
-        def swap(mask, _, chunk):
-            return flip(chunk, "row", n_row, mask)
-
-        def swap_first(mask, _, chunk):
-            return flip(chunk, "row", n_row, mask), half_grid(False)
+        def swap_first(mask, _, operands):
+            packed, slots = operands
+            packed = flip(packed, "row", n_row, mask)
+            mate_slots = flip(slots, "row", n_row, mask)
+            upper = place_ids >= half_rows * block_cols
+            mine = (slots >= 0) & (upper == (row < row_mate))
+            mates = (mate_slots >= 0) & (upper == (row > row_mate))
+            most = jnp.maximum(mine.astype(jnp.int32).sum(), mates.astype(jnp.int32).sum())
+            return packed, mate_slots, jnp.maximum(most - packed.shape[0], 0), half_grid(False)
 
         def swap_some(mask, count, singles):
             return [
@@ -366,24 +368,17 @@
         row_mate = row_partner[col, row]
         col_mate = col_partner[row, col]
 
-        mate_slots = pair_switch(row, row_mate, n_row, swap, slots)
-        upper = place_ids >= half_rows * block_cols
-        mine = (slots >= 0) & (upper == (row < row_mate))
-        mates = (mate_slots >= 0) & (upper == (row > row_mate))
-        most = jnp.maximum(mine.astype(jnp.int32).sum(), mates.astype(jnp.int32).sum())
-        extra = jnp.maximum(most - (half_rows * block_cols) // 2, 0)
-
         packed, *singles = half_grid(True)
-
-        packed, extra = lax.optimization_barrier((packed, extra))
-        packed, kept = pair_switch(row, row_mate, n_row, swap_first, packed)
-        counts = tuple(range(len(singles) + 1))
-        singles, packed = lax.optimization_barrier((singles, packed))
-        singles = pair_switch(row, row_mate, n_row, swap_some, singles, counts, extra)
+        packed, mate_slots, extra, kept = pair_switch(
+            row, row_mate, n_row, swap_first, (packed, slots)
+        )
         tables = (me, mate_slots, row_partner, col_partner)
         source = PackedSource(half_rows, block_cols)
-        section = sum_blocks(False, tables, source, kept[0], packed, singles)
+        section = sum_blocks(False, tables, source, kept[0], packed, [])
         section = pair_switch(col, col_mate, n_col, swap_section, section)
+        singles, section = lax.optimization_barrier((singles, section))
+        counts = tuple(range(len(singles) + 1))
+        singles = pair_switch(row, row_mate, n_row, swap_some, singles, counts, extra)
         return sum_blocks(True, tables, source, kept[1], packed, singles, section)
 
     in_specs = (

time: 198 us -> 174 us (0.88)
  the two profiles are of different devices: /device:TPU:11 before, /device:TPU:6 now
where the time goes in v1:
time: 174 us; the launch traced here: 176 us
  waiting for transfers between devices  97.9 us (56%)
  Pallas kernels  35.2 us (20%)
  starting transfers between devices  15.9 us (9%)
  between operations  15.4 us (9%)
  local copies, waits for them, and re-layouts  5.63 us (3%)
  other arithmetic  3.02 us (2%)
  loops' own time  2.7 us (2%)
    ppermute x9, waiting for transfers between devices, flip(): return lax.ppermute(value, axis, [(i, i ^ mask) for i in range(size)])  92.8 us
    pallas_call x2, Pallas kernels, left_products(): pl.pallas_call(functools.partial(left_kernel, given, half_rows, block_col...  15.5 us
    ppermute x9, starting transfers between devices, flip(): return lax.ppermute(value, axis, [(i, i ^ mask) for i in range(size)])  13.1 us
    pallas_call x2, Pallas kernels, right_products(): pl.pallas_call(functools.partial(right_kernel, given, block_cols, half_ro...  11.5 us
    pallas_call x2, Pallas kernels, sum_blocks(): pl.pallas_call(functools.partial(sum_kernel, source, first, len(singles))...  8.2 us
  transfers between devices with their start and end apart: 12, of which 9 were waited for; matrix products, arithmetic and copies ran while one was open for 5% of the time, Pallas kernels for 12%

profile of v1, /device:TPU:6, one launch (start us, length us, event | category | flops | bytes accessed | tf_op | source)
XLA Modules:
  0.0 175.8 jit_solution(3049188118877121542)
XLA Ops:
  6.5 0.7 all-gather.2.cloned.1.call-update
  7.3 2.7 %collective-permute-start.44 = (f32[512,256]{1,0:T(8,128)}, f32[512,256]{1,0:T(8,128)S(1)}, u32[]{:S(2)}, u32[]{:S(2)}) collective-permute-start(f32[512,256]{1,0:T(8,128)} %refs_5_.3), channel_id=1, source_target_pairs={{0,16},{8,24},{16,0},{24,8},{1,17},{9,25},{17,1},{25,9},{2,18},{10... | collective-permute-start | bytes 1572872 | tf_op jit(solution)/shard_map/ppermute | solution.py:300
  9.9 1.6 collective-permute-start.43
  11.5 1.5 collective-permute-start.45
  13.0 0.8 copy.16.refs_2_
  14.4 1.3 dynamic_slice.6
  16.3 1.3 dynamic_slice.7
  18.4 0.8 add_bitcast_fusion
  19.3 15.2 %collective-permute-done.44.refs_7_ = f32[512,256]{1,0:T(8,128)S(1)} collective-permute-done((f32[512,256]{1,0:T(8,128)}, f32[512,256]{1,0:T(8,128)S(1)}, u32[]{:S(2)}, u32[]{:S(2)}) %collective-permute-start.44) | collective-permute-done | bytes 524320 | tf_op jit(solution)/shard_map/ppermute | solution.py:300
  34.5 1.3 collective-permute-start.46
  35.8 1.6 all-gather.2.cloned.1.call-done.refs_3_
  37.4 7.9 %left_products.7.refs_4_ = bf16[4,2,512,512]{3,2,1,0:T(8,128)(2,1)S(1)} custom-call(s32[2]{0:T(128)S(1)} %pad_add_fusion.refs_0_, s32[16]{0:T(128)S(1)} %select_reduce_fusion.refs_1_, s32[8,4]{1,0:T(8,128)S(1)} %copy.16.refs_2_, f32[2048,256]{1,0:T(8,128)} %all-gather.2.cloned.1.call-done.refs_3_, f32[16,512,512]{2,1,0:T(8,128)} %refs_5_.2, ...), custom_call_target="tpu_custom_call" | custom-call | flops 6442450944 | bytes 12582912 | tf_op jit(solution)/shard_map/left_products/pallas_call | solution.py:82
  45.4 2.7 %collective-permute-done.46.refs_9_ = f32[512,256]{1,0:T(8,128)} collective-permute-done((f32[512,256]{1,0:T(8,128)S(1)}, f32[512,256]{1,0:T(8,128)}, u32[]{:S(2)}, u32[]{:S(2)}) %collective-permute-start.46) | collective-permute-done | bytes 524320 | tf_op jit(solution)/shard_map/ppermute | solution.py:310
  48.2 6.3 %right_products.7 = (f32[4,256,256]{2,1,0:T(8,128)}, f32[256,256]{1,0:T(8,128)}, f32[256,256]{1,0:T(8,128)}, f32[256,256]{1,0:T(8,128)}, f32[256,256]{1,0:T(8,128)S(1)}) custom-call(s32[2]{0:T(128)S(1)} %pad_add_fusion.refs_0_, s32[16]{0:T(128)S(1)} %select_reduce_fusion.refs_1_, s32[8,4]{1,0:T(8,128)S(1)} %copy.16.refs_2_, s32[4,8]{1,0:T(4,128)S(1)} %copy-done.2, ...), custom_call_target="tpu_custom_call" | custom-call | flops 1610612736 | bytes 6291456 | tf_op jit(solution)/shard_map/right_products/pallas_call | solution.py:215
  54.4 50.5 %conditional.3 = (f32[4,256,256]{2,1,0:T(8,128)}, s32[16]{0:T(128)}, s32[]{:T(128)}, f32[512,512]{1,0:T(8,128)S(1)}, f32[512,512]{1,0:T(8,128)S(1)}) conditional(s32[]{:T(128)} %clamp.9, (f32[4,256,256]{2,1,0:T(8,128)}, s32[16]{0:T(128)S(1)}, s32[16]{0:T(128)S(1)}, s32[16]{0:T(128)S(1)}, s32[]{:T(128)}, /*index=5*/s32[]{:T(128)}, ...), branch_computations={%region_1.4_spmd, %region_4.7_spmd, %region_7.10_spmd} | conditional | flops 8053063680 | bytes 23069624 | solution.py:318
  54.5 2.5 %collective-permute-start.39 = (f32[4,256,256]{2,1,0:T(8,128)}, f32[4,256,256]{2,1,0:T(8,128)}, u32[]{:S(2)}, u32[]{:S(2)}) collective-permute-start(f32[4,256,256]{2,1,0:T(8,128)} %get-tuple-element.251), channel_id=1, source_target_pairs={{0,16},{8,24},{16,0},{24,8},{1,17},{9,25},{17,1},{25,9},{2,18},{10... | collective-permute-start | bytes 3145736 | tf_op jit(solution)/shard_map/cond/branch_1_fun/ppermute | solution.py:300
  58.9 7.6 %left_products.5.refs_4_ = bf16[4,2,512,512]{3,2,1,0:T(8,128)(2,1)S(1)} custom-call(s32[2]{0:T(128)S(1)} %get-tuple-element.257.refs_0_, s32[16]{0:T(128)S(1)} %get-tuple-element.252.refs_1_, s32[8,4]{1,0:T(8,128)S(1)} %copy.18.refs_2_, f32[2048,256]{1,0:T(8,128)S(1)} %get-tuple-element.260.refs_3_, f32[16,512,512]{2,1,0:T(8,128)} %get-tuple-element.261.refs_4_.refs_5_, ...), custom_call_target="tpu_custom_call" | custom-call | flops 6442450944 | bytes 12582912 | tf_op jit(solution)/shard_map/cond/branch_1_fun/left_products/pallas_call | solution.py:82
  66.4 5.2 %right_products.5 = (f32[512,512]{1,0:T(8,128)S(1)}, f32[512,512]{1,0:T(8,128)S(1)}) custom-call(s32[2]{0:T(128)S(1)} %get-tuple-element.257.refs_0_, s32[16]{0:T(128)S(1)} %get-tuple-element.252.refs_1_, s32[8,4]{1,0:T(8,128)S(1)} %copy.18.refs_2_, s32[4,8]{1,0:T(4,128)S(1)} %get-tuple-element.259.refs_3_, ...), custom_call_target="tpu_custom_call" | custom-call | flops 1610612736 | bytes 6291456 | tf_op jit(solution)/shard_map/cond/branch_1_fun/right_products/pallas_call | solution.py:215
  72.3 29.9 %collective-permute-done.40 = s32[16]{0:T(128)} collective-permute-done((s32[16]{0:T(128)S(1)}, s32[16]{0:T(128)}, u32[]{:S(2)}, u32[]{:S(2)}) %collective-permute-start.40) | collective-permute-done | bytes 96 | tf_op jit(solution)/shard_map/cond/branch_1_fun/ppermute | solution.py:300
  102.2 1.4 fusion.3
  104.9 3.4 %sum_blocks.2 = f32[512,512]{1,0:T(8,128)S(1)} custom-call(s32[2]{0:T(128)S(1)} %pad_add_fusion.refs_0_, s32[16]{0:T(128)} %get-tuple-element.355.refs_1_, s32[8,4]{1,0:T(8,128)S(1)} %copy.16.refs_2_, s32[4,8]{1,0:T(4,128)S(1)} %copy-done.2, f32[512,512]{1,0:T(8,128)S(1)} %get-tuple-element.363.refs_4_, f32[4,256,256]{2,1,0:T(8,128)} %get-tuple-element.357.refs_5_), custom_call_target="tpu_custom_call" | custom-call | tf_op jit(solution)/shard_map/sum_blocks/pallas_call | solution.py:283
  108.3 24.1 %conditional.4 = (f32[512,512]{1,0:T(8,128)}) conditional(s32[]{:T(128)} %clamp.11, f32[512,512]{1,0:T(8,128)S(1)} %sum_blocks.2, f32[512,512]{1,0:T(8,128)S(1)} %sum_blocks.2, f32[512,512]{1,0:T(8,128)S(1)} %sum_blocks.2, f32[512,512]{1,0:T(8,128)S(1)} %sum_blocks.2, f32[512,512]{1,0:T(8,128)S(1)} %sum_blocks.2, ...), branch_computations={%region_10.11_spmd, %region_11.12_spmd, %region_12.13_spmd, %regio... | conditional | bytes 4194352 | solution.py:318
  108.4 24.0 %collective-permute-done.5 = f32[512,512]{1,0:T(8,128)} collective-permute-done((f32[512,512]{1,0:T(8,128)S(1)}, f32[512,512]{1,0:T(8,128)}, u32[]{:S(2)}, u32[]{:S(2)}) %collective-permute-start.5) | collective-permute-done | bytes 1048608 | tf_op jit(solution)/shard_map/cond/branch_5_fun/ppermute | solution.py:300
  132.4 31.7 %conditional.5 = ((f32[256,256]{1,0:T(8,128)}, f32[256,256]{1,0:T(8,128)}, f32[256,256]{1,0:T(8,128)}, f32[256,256]{1,0:T(8,128)S(1)})) conditional(s32[]{:T(128)} %clamp.10, (f32[256,256]{1,0:T(8,128)}, f32[256,256]{1,0:T(8,128)}, f32[256,256]{1,0:T(8,128)}, f32[256,256]{1,0:T(8,128)S(1)}) %tuple.98, ...), branch_computations={%region_17.18_spmd, %region_18.19_spmd, %region_19.20_spmd, %regio... | conditional | bytes 6291656 | solution.py:318
  132.4 2.9 %collective-permute-start.24 = (f32[256,256]{1,0:T(8,128)}, f32[256,256]{1,0:T(8,128)S(1)}, u32[]{:S(2)}, u32[]{:S(2)}) collective-permute-start(f32[256,256]{1,0:T(8,128)} %get-tuple-element.316), channel_id=1, source_target_pairs={{0,16},{8,24},{16,0},{24,8},{1,17},{9,25},{17,1},{25,9},{2,18},{10... | collective-permute-start | bytes 786440 | tf_op jit(solution)/shard_map/cond/branch_9_fun/ppermute | solution.py:300
  135.4 2.9 %collective-permute-start.26 = (f32[256,256]{1,0:T(8,128)S(1)}, f32[256,256]{1,0:T(8,128)S(1)}, u32[]{:S(2)}, u32[]{:S(2)}) collective-permute-start(f32[256,256]{1,0:T(8,128)S(1)} %get-tuple-element.318), channel_id=1, source_target_pairs={{0,16},{8,24},{16,0},{24,8},{1,17},{9,25},{17,1},{25,9},{2,18},{10... | collective-permute-start | bytes 786440 | tf_op jit(solution)/shard_map/cond/branch_9_fun/ppermute | solution.py:300
  138.3 12.9 %collective-permute-done.23 = f32[256,256]{1,0:T(8,128)S(1)} collective-permute-done((f32[256,256]{1,0:T(8,128)}, f32[256,256]{1,0:T(8,128)S(1)}, u32[]{:S(2)}, u32[]{:S(2)}) %collective-permute-start.23) | collective-permute-done | bytes 262176 | tf_op jit(solution)/shard_map/cond/branch_9_fun/ppermute | solution.py:300
  151.2 0.7 copy.80
  151.9 4.9 %collective-permute-done.24 = f32[256,256]{1,0:T(8,128)S(1)} collective-permute-done((f32[256,256]{1,0:T(8,128)}, f32[256,256]{1,0:T(8,128)S(1)}, u32[]{:S(2)}, u32[]{:S(2)}) %collective-permute-start.24) | collective-permute-done | bytes 262176 | tf_op jit(solution)/shard_map/cond/branch_9_fun/ppermute | solution.py:300
  157.6 3.7 %collective-permute-done.25 = f32[256,256]{1,0:T(8,128)S(1)} collective-permute-done((f32[256,256]{1,0:T(8,128)}, f32[256,256]{1,0:T(8,128)S(1)}, u32[]{:S(2)}, u32[]{:S(2)}) %collective-permute-start.25) | collective-permute-done | bytes 262176 | tf_op jit(solution)/shard_map/cond/branch_9_fun/ppermute | solution.py:300
  162.0 2.1 %collective-permute-done.26 = f32[256,256]{1,0:T(8,128)S(1)} collective-permute-done((f32[256,256]{1,0:T(8,128)S(1)}, f32[256,256]{1,0:T(8,128)S(1)}, u32[]{:S(2)}, u32[]{:S(2)}) %collective-permute-start.26) | collective-permute-done | bytes 262176 | tf_op jit(solution)/shard_map/cond/branch_9_fun/ppermute | solution.py:300
  164.1 4.8 %sum_blocks.3 = f32[512,512]{1,0:T(8,128)} custom-call(s32[2]{0:T(128)S(1)} %pad_add_fusion.refs_0_, s32[16]{0:T(128)} %get-tuple-element.355.refs_1_, s32[8,4]{1,0:T(8,128)S(1)} %copy.16.refs_2_, s32[4,8]{1,0:T(4,128)S(1)} %copy-done.2, f32[512,512]{1,0:T(8,128)S(1)} %get-tuple-element.356.refs_4_, f32[4,256,256]{2,1,0:T(8,128)} %get-tuple-element.357.refs_5_, ...), custom_call_target="tpu_custom_call" | custom-call | tf_op jit(solution)/shard_map/sum_blocks/pallas_call | solution.py:283
  (25 shorter events, 3.0 us)
Async XLA Ops:
  6.5 30.9 %all-gather.2.cloned.1.call-start = ((), (), s32[]{:S(2)}) async-start(), calls=%async_computation | async-start | bytes 2359296 | tf_op jit(solution)/shard_map/all_gather | solution.py:334
  7.3 27.2 %collective-permute-start.44 = (f32[512,256]{1,0:T(8,128)}, f32[512,256]{1,0:T(8,128)S(1)}, u32[]{:S(2)}, u32[]{:S(2)}) collective-permute-start(f32[512,256]{1,0:T(8,128)} %refs_5_.3), channel_id=1, source_target_pairs={{0,16},{8,24},{16,0},{24,8},{1,17},{9,25},{17,1},{25,9},{2,18},{10... | collective-permute-start | bytes 1572872 | tf_op jit(solution)/shard_map/ppermute | solution.py:300
  9.9 35.5 %collective-permute-start.43 = (f32[512,256]{1,0:T(8,128)}, f32[512,256]{1,0:T(8,128)}, u32[]{:S(2)}, u32[]{:S(2)}) collective-permute-start(f32[512,256]{1,0:T(8,128)} %refs_5_.3), channel_id=1, source_target_pairs={{0,8},{8,0},{16,24},{24,16},{1,9},{9,1},{17,25},{25,17},{2,10},{10... | collective-permute-start | bytes 1572872 | tf_op jit(solution)/shard_map/ppermute | solution.py:300
  11.5 33.9 %collective-permute-start.45 = (f32[512,256]{1,0:T(8,128)}, f32[512,256]{1,0:T(8,128)}, u32[]{:S(2)}, u32[]{:S(2)}) collective-permute-start(f32[512,256]{1,0:T(8,128)} %refs_5_.3), channel_id=1, source_target_pairs={{8,16},{16,8},{9,17},{17,9},{10,18},{18,10},{11,19},{19,11},{12,20... | collective-permute-start | bytes 1572872 | tf_op jit(solution)/shard_map/ppermute | solution.py:309
  19.2 28.9 %copy-start.1 = (f32[512,256]{1,0:T(8,128)S(1)}, f32[512,256]{1,0:T(8,128)}, u32[]{:S(2)}) copy-start(f32[512,256]{1,0:T(8,128)} %refs_5_.3) | copy-start | bytes 1572868
  19.3 28.9 %copy-start.2 = (s32[4,8]{1,0:T(4,128)S(1)}, s32[4,8]{1,0:T(4,128)}, u32[]{:S(2)}) copy-start(s32[4,8]{1,0:T(4,128)} %refs_3_.5) | copy-start | bytes 388
  34.5 13.7 %collective-permute-start.46 = (f32[512,256]{1,0:T(8,128)S(1)}, f32[512,256]{1,0:T(8,128)}, u32[]{:S(2)}, u32[]{:S(2)}) collective-permute-start(f32[512,256]{1,0:T(8,128)S(1)} %collective-permute-done.44.refs_7_), channel_id=1, source_target_pairs={{8,0},{16,24},{9,1},{17,25},{10,2},{18,26},{11,3},{19,27},{12,4},{... | collective-permute-start | bytes 1572872 | tf_op jit(solution)/shard_map/ppermute | solution.py:310
  45.4 9.1 %copy-start = (f32[2048,256]{1,0:T(8,128)S(1)}, f32[2048,256]{1,0:T(8,128)}, u32[]{:S(2)}) copy-start(f32[2048,256]{1,0:T(8,128)} %all-gather.2.cloned.1.call-done.refs_3_) | copy-start | bytes 6291460
  45.4 9.0 %copy-start.3 = (s32[8,4]{0,1:T(4,128)S(1)}, s32[8,4]{0,1:T(4,128)}, u32[]{:S(2)}) copy-start(s32[8,4]{0,1:T(4,128)} %param.37) | copy-start | bytes 388
  54.5 50.4 %collective-permute-start.39 = (f32[4,256,256]{2,1,0:T(8,128)}, f32[4,256,256]{2,1,0:T(8,128)}, u32[]{:S(2)}, u32[]{:S(2)}) collective-permute-start(f32[4,256,256]{2,1,0:T(8,128)} %get-tuple-element.251), channel_id=1, source_target_pairs={{0,16},{8,24},{16,0},{24,8},{1,17},{9,25},{17,1},{25,9},{2,18},{10... | collective-permute-start | bytes 3145736 | tf_op jit(solution)/shard_map/cond/branch_1_fun/ppermute | solution.py:300
  57.0 45.2 %collective-permute-start.40 = (s32[16]{0:T(128)S(1)}, s32[16]{0:T(128)}, u32[]{:S(2)}, u32[]{:S(2)}) collective-permute-start(s32[16]{0:T(128)S(1)} %get-tuple-element.252.refs_1_), channel_id=1, source_target_pairs={{0,16},{8,24},{16,0},{24,8},{1,17},{9,25},{17,1},{25,9},{2,18},{10... | collective-permute-start | bytes 200 | tf_op jit(solution)/shard_map/cond/branch_1_fun/ppermute | solution.py:300
  108.4 24.1 %collective-permute-start.5 = (f32[512,512]{1,0:T(8,128)S(1)}, f32[512,512]{1,0:T(8,128)}, u32[]{:S(2)}, u32[]{:S(2)}) collective-permute-start(f32[512,512]{1,0:T(8,128)S(1)} %param.8), channel_id=1, source_target_pairs={{0,6},{1,7},{2,4},{3,5},{4,2},{5,3},{6,0},{7,1},{8,14},{9,15},{10,... | collective-permute-start | bytes 3145736 | tf_op jit(solution)/shard_map/cond/branch_5_fun/ppermute | solution.py:300
  132.4 18.8 %collective-permute-start.23 = (f32[256,256]{1,0:T(8,128)}, f32[256,256]{1,0:T(8,128)S(1)}, u32[]{:S(2)}, u32[]{:S(2)}) collective-permute-start(f32[256,256]{1,0:T(8,128)} %get-tuple-element.315), channel_id=1, source_target_pairs={{0,16},{8,24},{16,0},{24,8},{1,17},{9,25},{17,1},{25,9},{2,18},{10... | collective-permute-start | bytes 786440 | tf_op jit(solution)/shard_map/cond/branch_9_fun/ppermute | solution.py:300
  132.4 24.4 %collective-permute-start.24 = (f32[256,256]{1,0:T(8,128)}, f32[256,256]{1,0:T(8,128)S(1)}, u32[]{:S(2)}, u32[]{:S(2)}) collective-permute-start(f32[256,256]{1,0:T(8,128)} %get-tuple-element.316), channel_id=1, source_target_pairs={{0,16},{8,24},{16,0},{24,8},{1,17},{9,25},{17,1},{25,9},{2,18},{10... | collective-permute-start | bytes 786440 | tf_op jit(solution)/shard_map/cond/branch_9_fun/ppermute | solution.py:300
  135.4 25.9 %collective-permute-start.25 = (f32[256,256]{1,0:T(8,128)}, f32[256,256]{1,0:T(8,128)S(1)}, u32[]{:S(2)}, u32[]{:S(2)}) collective-permute-start(f32[256,256]{1,0:T(8,128)} %get-tuple-element.317), channel_id=1, source_target_pairs={{0,16},{8,24},{16,0},{24,8},{1,17},{9,25},{17,1},{25,9},{2,18},{10... | collective-permute-start | bytes 786440 | tf_op jit(solution)/shard_map/cond/branch_9_fun/ppermute | solution.py:300
  135.4 28.7 %collective-permute-start.26 = (f32[256,256]{1,0:T(8,128)S(1)}, f32[256,256]{1,0:T(8,128)S(1)}, u32[]{:S(2)}, u32[]{:S(2)}) collective-permute-start(f32[256,256]{1,0:T(8,128)S(1)} %get-tuple-element.318), channel_id=1, source_target_pairs={{0,16},{8,24},{16,0},{24,8},{1,17},{9,25},{17,1},{25,9},{2,18},{10... | collective-permute-start | bytes 786440 | tf_op jit(solution)/shard_map/cond/branch_9_fun/ppermute | solution.py:300
Sparse Core Ops, SparseCore 0:
  9.2 28.1 all-gather.1
